TPU v7x, 256 devices: a whole 4x4x8 slice. The times are simulated.
256 devices in a mesh: seed: 4 (over x), fsdp: 8 (over y, core), seq: 8 (over z).
Axes of the slice: x: 4, y: 4, z: 8, core: 2. Of those that a mesh axis runs over, the one named last changes fastest.
Arguments:
- mel_frames: bfloat16 [8, 32768, 80], P('fsdp', 'seq'), may hold values from -6 to 6
- lengths: int32 [8], P('fsdp'), may hold values from 1 to 8192, 40960 in all
- targets: int32 [8, 8192], P('fsdp', 'seq'), may hold values from 0 to 511
- frame_mask: int32 [8, 8192], P('fsdp', 'seq'), may hold values 0 or 1
- stem_weight: bfloat16 [4, 640, 1536], P('seed'), may hold values from -0.25 to 0.25
- conv_in_weight: bfloat16 [4, 1536, 1536], P('seed', ('fsdp', 'seq')), may hold values from -0.15625 to 0.15625
- conv_out_weight: bfloat16 [4, 768, 1536], P('seed', ('fsdp', 'seq')), may hold values from -0.21875 to 0.21875
- depth_weight: bfloat16 [4, 31, 768], P('seed'), may hold values from -1 to 1
- head_weight: bfloat16 [4, 1536, 512], P('seed', ('fsdp', 'seq')), may hold values from -80 to 80
- norm_gain: float32 [4, 2, 1536], P('seed'), may hold values from 0.5 to 1.5
Outputs:
- frame_error: float32 [8, 8192], P('fsdp', 'seq')
- utt_score: float32 [8], P('fsdp')
Inputs may be any that keep to these rules, and one draw needn't show every extreme that they name: `lengths`: some utterance has exactly 8192 valid frames.
All inputs are finite; a program needn't handle non-finite values. No bound on the sum of `lengths` or of `frame_mask` on one device may be relied on, other than what follows from the above.
Results may differ from a plain program's by a relative error of at most 0.0022.
Values may be sent and summed in bfloat16 or wider, within the bound.
A program may use at most 64 MiB of HBM per device.

v0:
```python
import jax
import jax.numpy as jnp
from jax import lax
from jax.sharding import PartitionSpec as P


def from_behind(x, axis, by):
    count = lax.axis_size(axis)
    pairs = [(i, i + by) for i in range(count) if 0 <= i + by < count]
    return lax.ppermute(x, axis, pairs)


def extended(x, sides, width):
    for axis, dim in sides:
        count, length = (lax.axis_size(axis), x.shape[dim])
        up = [(i, (i + 1) % count) for i in range(count - 1)]
        down = [(j, i) for i, j in up]
        last = lax.slice_in_dim(x, length - width, length, axis=dim)
        first = lax.slice_in_dim(x, 0, width, axis=dim)
        before = lax.ppermute(last, axis, up)
        after = lax.ppermute(first, axis, down)
        x = jnp.concatenate([before, x, after], axis=dim)
    return x


def layer_norm(values, gain_row):
    row_mean = jnp.mean(values, axis=-1, keepdims=True)
    centred = values - row_mean
    row_var = jnp.mean(centred * centred, axis=-1, keepdims=True)
    return (centred * lax.rsqrt(row_var + 1e-05) * gain_row).astype(jnp.bfloat16)


def block_product(left_rows, right_matrix):
    return jnp.dot(left_rows, right_matrix, preferred_element_type=jnp.float32)


def row_product(activations, shard_piece):
    return block_product(activations, shard_piece[0])


def body(
    mel_frames,
    lengths,
    targets,
    frame_mask,
    stem_weight,
    conv_in_weight,
    conv_out_weight,
    depth_weight,
    head_weight,
    norm_gain,
):
    frame_rows = targets.shape[1]
    blocks = mel_frames[0].reshape(frame_rows, -1)
    next_block = from_behind(blocks[:1], "seq", -1)
    following = jnp.concatenate([blocks[1:], next_block], 0)
    half_width = blocks.shape[1]
    stem_matrix = stem_weight[0]
    stem_out = (
        jnp.dot(blocks, stem_matrix[:half_width], preferred_element_type=jnp.float32)
        + jnp.dot(following, stem_matrix[half_width:], preferred_element_type=jnp.float32)
    ).astype(jnp.bfloat16)
    offset = lax.axis_index("seq") * frame_rows
    length = lengths[0]
    positions = offset + jnp.arange(frame_rows, dtype=jnp.int32)
    frame_live = positions < length
    gain_rows = norm_gain[0]
    normed_one = layer_norm(stem_out.astype(jnp.float32), gain_rows[0])
    tap_count = depth_weight.shape[1]
    channels = depth_weight.shape[2]
    halo_width = tap_count // 2
    mixed_rows = row_product(
        normed_one, lax.all_gather(conv_in_weight, ("fsdp", "seq"), axis=1, tiled=True)
    )
    input_positions = offset + jnp.arange(normed_one.shape[0], dtype=jnp.int32)
    input_live = jnp.logical_and(input_positions >= 0, input_positions < length)
    gated_rows = (
        mixed_rows[:, :channels]
        * jax.nn.sigmoid(mixed_rows[:, channels:])
        * input_live[:, None].astype(jnp.float32)
    ).astype(jnp.bfloat16)
    padded = extended(gated_rows, (("seq", 0),), halo_width)
    depthwise = jnp.zeros((frame_rows, channels), jnp.float32)
    for tap_index in range(tap_count):
        depthwise = depthwise + padded[tap_index : tap_index + frame_rows].astype(
            jnp.float32
        ) * depth_weight[0, tap_index].astype(jnp.float32)
    swished = jax.nn.silu(depthwise).astype(jnp.bfloat16)
    conv_proj = row_product(
        swished, lax.all_gather(conv_out_weight, ("fsdp", "seq"), axis=1, tiled=True)
    )
    after_conv = stem_out.astype(jnp.float32) + conv_proj
    normed_two = layer_norm(after_conv, gain_rows[1])
    logits = row_product(
        normed_two, lax.all_gather(head_weight, ("fsdp", "seq"), axis=1, tiled=True)
    )
    posterior = jax.nn.softmax(logits, axis=-1)
    vocab_size = logits.shape[1]
    onehot = (jnp.arange(vocab_size, dtype=jnp.int32)[None, :] == targets[0][:, None]).astype(
        jnp.float32
    )
    differ = posterior - onehot
    frame_err = (
        jnp.sqrt(jnp.sum(differ * differ, axis=-1))
        * frame_live.astype(jnp.float32)
        * frame_mask[0].astype(jnp.float32)
    )
    seed_count = lax.axis_size("seed")
    frame_error = lax.psum(frame_err, "seed") / jnp.float32(seed_count)
    numerator = lax.psum(jnp.sum(frame_error), "seq")
    utt_score = numerator / length.astype(jnp.float32)
    return (frame_error[None, :], utt_score.reshape(1))


def solution(mesh):
    in_specs = (
        P("fsdp", "seq", None),
        P("fsdp"),
        P("fsdp", "seq"),
        P("fsdp", "seq"),
        P("seed", None, None),
        P("seed", ("fsdp", "seq"), None),
        P("seed", ("fsdp", "seq"), None),
        P("seed", None, None),
        P("seed", ("fsdp", "seq"), None),
        P("seed", None, None),
    )
    out_specs = (P("fsdp", "seq"), P("fsdp"))
    return jax.shard_map(body, mesh=mesh, in_specs=in_specs, out_specs=out_specs, check_vma=False)
```

profile of v0, /device:TPU:8, one launch (start us, length us, event | category | flops | bytes accessed | tf_op | source)
XLA Modules:
  0.0 291.0 jit_solution(8486558325888110013)
XLA Ops:
  7.2 0.0 copy-start.3
  7.2 0.0 all-gather.4.cloned.1.call-start
  7.2 0.7 all-gather.4.cloned.1.call-update
  7.9 0.0 all-gather.6.cloned.1.call-start
  8.0 1.5 copy.22
  9.4 0.0 all-gather.6.cloned.1.call-update
  9.5 0.0 all-gather.8.cloned.1.call-start
  9.5 0.7 slice.261
  10.2 0.1 copy.21
  10.3 0.1 slice.262
  10.4 1.3 collective-permute-start
  11.7 0.0 all-gather.8.cloned.1.call-update
  11.7 1.6 copy.19
  13.3 1.4 convert_reduce_fusion.31
  14.8 0.7 reshape_squeeze.3
  15.4 0.0 copy-done.3
  16.1 0.0 copy-start
  16.2 5.7 %fusion.54 = f32[1024,1536]{1,0:T(8,128)} fusion(bf16[1024,320]{1,0:T(8,128)(2,1)S(1)} %reshape_squeeze.3, bf16[1,640,1536]{2,1,0:T(8,128)(2,1)} %param.14), kind=kOutput, calls=%fused_computation.110 | convolution fusion | flops 1006632960 | bytes 7929856 | tf_op jit(solution)/shard_map/dot_general | solution.py:60
  21.9 0.0 copy-done
  21.9 0.2 slice.259
  22.1 0.6 copy.20
  22.8 1.6 slice.260
  24.4 0.0 collective-permute-done
  24.4 5.3 %convert_reduce_fusion = (f32[1024]{0:T(1024)S(1)}, bf16[1024,1536]{1,0:T(8,128)(2,1)S(1)}) fusion(f32[1024,1536]{1,0:T(8,128)} %fusion.54, bf16[1,640,1536]{2,1,0:T(8,128)(2,1)} %param.14, bf16[1,320]{1,0:T(2,128)(2,1)S(1)} %collective-permute-done, bf16[1023,320]{1,0:T(8,128)(2,1)} %slice.260), kind=kOutput, calls=%fused_computation.2 | convolution fusion | flops 1014234112 | bytes 11211392 | tf_op jit(solution)/shard_map/dot_general | solution.py:61
  29.7 1.0 fusion.2
  30.7 61.1 %all-gather.4.cloned.1.call-done = bf16[1,1536,1536]{2,1,0:T(8,128)(2,1)} async-done(((bf16[1,24,1536]{2,1,0:T(8,128)(2,1)}), bf16[1,1536,1536]{2,1,0:T(8,128)(2,1)}) %all-gather.4.cloned.1.call-update) | async-done | bytes 4718608 | tf_op jit(solution)/shard_map/all_gather | solution.py:73
  91.7 7.2 %fusion.5 = f32[1024,1536]{1,0:T(8,128)S(1)} fusion(bf16[1,1536,1536]{2,1,0:T(8,128)(2,1)} %all-gather.4.cloned.1.call-done, bf16[1024,1536]{1,0:T(8,128)(2,1)S(1)} %get-tuple-element.40, f32[1536]{0:T(1024)S(1)} %get-tuple-element.34, f32[1024]{0:T(1024)S(1)} %add_rsqrt_fusion.1, f32[1024]{0:T(1024)S(1)} %broadcast_multiply_fusion.2), kind=kOutput, calls=%fused_computation.39 | convolution fusion | flops 4839702528 | bytes 14170112 | tf_op jit(solution)/shard_map/dot_general | solution.py:34
  99.0 0.0 copy-start.2
  99.0 0.0 copy-start.5
  99.0 0.8 fusion.20
  99.9 0.0 copy-start.1
  99.9 1.1 copy-done.1
  101.0 3.1 %collective-permute-start.1 = (bf16[15,768]{1,0:T(8,128)(2,1)S(1)}, bf16[15,768]{1,0:T(8,128)(2,1)S(1)}, u32[]{:S(2)}, u32[]{:S(2)}) collective-permute-start(bf16[15,768]{1,0:T(8,128)(2,1)S(1)} %get-tuple-element.35), channel_id=1, source_target_pairs={{0,1},{1,2},{2,3},{3,4},{4,5},{5,6},{6,7},{8,9},{9,10},{10,11},{11... | collective-permute-start | bytes 69128 | tf_op jit(solution)/shard_map/ppermute | solution.py:20
  104.1 1.5 collective-permute-start.2
  105.6 0.0 copy-done.2
  105.6 0.1 convert_reduce_fusion.30
  105.7 0.0 copy-done.5
  105.8 65.5 %all-gather.6.cloned.1.call-done = bf16[1,768,1536]{2,0,1:T(2,128)(2,1)} async-done(((bf16[1,12,1536]{2,0,1:T(2,128)(2,1)}), bf16[1,768,1536]{2,0,1:T(2,128)(2,1)}) %all-gather.6.cloned.1.call-update) | async-done | bytes 2359312 | tf_op jit(solution)/shard_map/all_gather | solution.py:90
  171.3 0.0 collective-permute-done.1
  171.3 0.0 collective-permute-done.2
  171.3 48.2 %fusion.70 = (f32[1024]{0:T(1024)S(1)}, f32[1024,1536]{1,0:T(8,128)}) fusion(bf16[1,768,1536]{2,0,1:T(2,128)(2,1)} %all-gather.6.cloned.1.call-done, bf16[1024,768]{1,0:T(8,128)(2,1)} %copy-done.1, bf16[15,768]{1,0:T(8,128)(2,1)S(1)} %collective-permute-done.2, bf16[15,768]{1,0:T(8,128)(2,1)S(1)} %collective-permute-done.1, ...), kind=kOutput, calls=%fused_computation.166 | convolution fusion | flops 2567699456 | bytes 13514752 | tf_op jit(solution)/shard_map/dot_general | solution.py:34
  219.5 3.6 %multiply_reduce_fusion = f32[1024]{0:T(1024)S(1)} fusion(f32[1024,1536]{1,0:T(8,128)} %get-tuple-element.42, f32[1024]{0:T(1024)S(1)} %broadcast_multiply_fusion.1), kind=kLoop, calls=%fused_computation.37 | loop fusion | flops 4717568 | bytes 6299648 | tf_op jit(solution)/shard_map/reduce_sum | solution.py:29
  223.1 25.5 %all-gather.8.cloned.1.call-done = bf16[1,1536,512]{2,1,0:T(8,128)(2,1)} async-done(((bf16[1,24,512]{2,1,0:T(8,128)(2,1)}), bf16[1,1536,512]{2,1,0:T(8,128)(2,1)}) %all-gather.8.cloned.1.call-update) | async-done | bytes 1572880 | tf_op jit(solution)/shard_map/all_gather | solution.py:95
  248.6 0.0 copy-start.4
  248.6 5.0 %fusion.71 = (f32[1024]{0:T(1024)S(1)}, f32[1024,512]{0,1:T(8,128)S(1)}) fusion(bf16[1,1536,512]{2,1,0:T(8,128)(2,1)} %all-gather.8.cloned.1.call-done, f32[1024,1536]{1,0:T(8,128)} %get-tuple-element.42, f32[1536]{0:T(1024)S(1)} %get-tuple-element.33, f32[1024]{0:T(1024)S(1)} %add_rsqrt_fusion, f32[1024]{0:T(1024)S(1)} %broadcast_multiply_fusion.1), kind=kOutput, calls=%fused_computation.167 | convolution fusion | flops 1617427456 | bytes 9979904 | tf_op jit(solution)/shard_map/dot_general | solution.py:34
  253.6 0.3 fusion.23
  254.0 0.0 copy-done.4
  254.0 0.7 multiply_reduce_fusion.1
  254.7 10.4 %psum.14 = f32[1024]{0:T(1024)S(1)} all-reduce(f32[1024]{0:T(1024)S(1)} %select_multiply_fusion), channel_id=1, replica_groups=mesh['seed'=4,'fsdp'=8,'seq'=8] {'seed'}, use_global_device_ids=true, to_apply=%region_7.8 | all-reduce | flops 1024 | bytes 8192 | tf_op jit(solution)/shard_map/psum | solution.py:109
  265.1 1.2 fusion.68
  266.3 16.4 %psum.15 = f32[]{:T(128)} all-reduce(f32[]{:T(128)} %get-tuple-element.37), channel_id=1, replica_groups=mesh['seed'=4,'fsdp'=8,'seq'=8] {'seq'}, use_global_device_ids=true, to_apply=%region_9.10 | all-reduce | flops 1 | bytes 8 | tf_op jit(solution)/shard_map/psum | solution.py:110
  (9 shorter events, 0.1 us)
Async XLA Ops:
  7.2 8.3 %copy-start.3 = (f32[1,2,1536]{2,1,0:T(2,128)S(1)}, f32[1,2,1536]{2,1,0:T(2,128)}, u32[]{:S(2)}) copy-start(f32[1,2,1536]{2,1,0:T(2,128)} %param.19) | copy-start | bytes 36868
  7.2 84.6 %all-gather.4.cloned.1.call-start = ((), (), s32[]{:S(2)}) async-start(), calls=%async_computation | async-start | bytes 4792320 | tf_op jit(solution)/shard_map/all_gather | solution.py:73
  7.9 163.4 %all-gather.6.cloned.1.call-start = ((), (), s32[]{:S(2)}) async-start(), calls=%async_computation.1 | async-start | bytes 4792320 | tf_op jit(solution)/shard_map/all_gather | solution.py:90
  9.5 239.1 %all-gather.8.cloned.1.call-start = ((), (), s32[]{:S(2)}) async-start(), calls=%async_computation.2 | async-start | bytes 1597440 | tf_op jit(solution)/shard_map/all_gather | solution.py:95
  10.4 14.0 %collective-permute-start = (bf16[1,320]{1,0:T(2,128)(2,1)S(1)}, bf16[1,320]{1,0:T(2,128)(2,1)S(1)}, u32[]{:S(2)}, u32[]{:S(2)}) collective-permute-start(bf16[1,320]{1,0:T(2,128)(2,1)S(1)} %slice.262), channel_id=1, source_target_pairs={{1,0},{2,1},{3,2},{4,3},{5,4},{6,5},{7,6},{9,8},{10,9},{11,10},{12... | collective-permute-start | bytes 1928 | tf_op jit(solution)/shard_map/ppermute | solution.py:10
  16.1 5.7 %copy-start = (bf16[1,4096,80]{1,2,0:T(8,128)(2,1)S(1)}, bf16[1,4096,80]{1,2,0:T(8,128)(2,1)}, u32[]{:S(2)}) copy-start(bf16[1,4096,80]{1,2,0:T(8,128)(2,1)} %param.10) | copy-start | bytes 1966084
  99.0 6.6 %copy-start.2 = (bf16[1,31,768]{2,1,0:T(8,128)(2,1)S(1)}, bf16[1,31,768]{2,1,0:T(8,128)(2,1)}, u32[]{:S(2)}) copy-start(bf16[1,31,768]{2,1,0:T(8,128)(2,1)} %param.17) | copy-start | bytes 142852
  99.0 6.7 %copy-start.5 = (s32[1,1024]{1,0:T(1,128)S(1)}, s32[1,1024]{1,0:T(1,128)}, u32[]{:S(2)}) copy-start(s32[1,1024]{1,0:T(1,128)} %param.13) | copy-start | bytes 12292
  99.9 1.1 copy-start.1
  101.0 70.3 %collective-permute-start.1 = (bf16[15,768]{1,0:T(8,128)(2,1)S(1)}, bf16[15,768]{1,0:T(8,128)(2,1)S(1)}, u32[]{:S(2)}, u32[]{:S(2)}) collective-permute-start(bf16[15,768]{1,0:T(8,128)(2,1)S(1)} %get-tuple-element.35), channel_id=1, source_target_pairs={{0,1},{1,2},{2,3},{3,4},{4,5},{5,6},{6,7},{8,9},{9,10},{10,11},{11... | collective-permute-start | bytes 69128 | tf_op jit(solution)/shard_map/ppermute | solution.py:20
  104.1 67.1 %collective-permute-start.2 = (bf16[15,768]{1,0:T(8,128)(2,1)S(1)}, bf16[15,768]{1,0:T(8,128)(2,1)S(1)}, u32[]{:S(2)}, u32[]{:S(2)}) collective-permute-start(bf16[15,768]{1,0:T(8,128)(2,1)S(1)} %get-tuple-element.36), channel_id=1, source_target_pairs={{1,0},{2,1},{3,2},{4,3},{5,4},{6,5},{7,6},{9,8},{10,9},{11,10},{12... | collective-permute-start | bytes 69128 | tf_op jit(solution)/shard_map/ppermute | solution.py:21
  248.6 5.4 %copy-start.4 = (s32[1,1024]{1,0:T(1,128)S(1)}, s32[1,1024]{1,0:T(1,128)}, u32[]{:S(2)}) copy-start(s32[1,1024]{1,0:T(1,128)} %param.12) | copy-start | bytes 12292
Sparse Core Ops, SparseCore 0:
  10.8 80.9 all-gather.3
  94.5 76.7 all-gather.5
  174.0 74.5 all-gather.7
where the time goes:
time: 291 us
  waiting for transfers between devices  153 us (53%)
  matrix products  71.4 us (25%)
  blocking collectives  26.8 us (9%)
  between operations  16.4 us (6%)
  other arithmetic  9.23 us (3%)
  local copies, waits for them, and re-layouts  8.3 us (3%)
  starting transfers between devices  6 us (2%)
    all_gather x1, waiting for transfers between devices, body(): lax.all_gather(conv_out_weight, ('fsdp', 'seq'), axis=1, tiled=True)  65.5 us
    all_gather x1, waiting for transfers between devices, body(): lax.all_gather(conv_in_weight, ('fsdp', 'seq'), axis=1, tiled=True)  61.1 us
    dot_general x3, matrix products, block_product(): return jnp.dot(left_rows, right_matrix, preferred_element_type=jnp.float32)  60.4 us
    all_gather x1, waiting for transfers between devices, body(): lax.all_gather(head_weight, ('fsdp', 'seq'), axis=1, tiled=True)  25.5 us
    psum x1, blocking collectives, body(): numerator = lax.psum(jnp.sum(frame_error), 'seq')  16.4 us
    psum x1, blocking collectives, body(): frame_error = lax.psum(frame_err, 'seed') / jnp.float32(seed_count)  10.4 us
  transfers between devices with their start and end apart: 6, of which 3 were waited for; matrix products, arithmetic and copies ran while one was open for 28% of the time, Pallas kernels for 0%

commit v1 on v0

--- a/solution.py
+++ b/solution.py
@@ -92,7 +92,13 @@
     after_conv = stem_out.astype(jnp.float32) + conv_proj
     normed_two = layer_norm(after_conv, gain_rows[1])
     logits = row_product(
-        normed_two, lax.all_gather(head_weight, ("fsdp", "seq"), axis=1, tiled=True)
+        normed_two,
+        jnp.concatenate(
+            lax.all_to_all(
+                jnp.stack([head_weight] * lax.axis_size(("fsdp", "seq"))), ("fsdp", "seq"), 0, 0
+            ),
+            axis=1,
+        ),
     )
     posterior = jax.nn.softmax(logits, axis=-1)
     vocab_size = logits.shape[1]

time: 291 us -> 271 us (0.931)
  waiting for transfers between devices: 153 us -> 118 us
  starting transfers between devices: 6 us -> 19.5 us
    all_gather x1 -> x0, waiting for transfers between devices: 25.5 us -> none  [body(): lax.all_gather(head_weight, ('fsdp', 'seq'), axis=1, tiled=True)]
    all_to_all x0 -> x1, starting transfers between devices: none -> 13.6 us  [body(): lax.all_to_all(jnp.stack([head_weight] * lax.axis_size(('fsdp', 'seq'))),...]
    all_gather x1, waiting for transfers between devices: 61.1 us -> 52 us  [body(): lax.all_gather(conv_in_weight, ('fsdp', 'seq'), axis=1, tiled=True)]
  transfers between devices with their start and end apart: 6 -> 6, of which waited for: 3 -> 2; matrix products, arithmetic and copies ran while one was open for 28% -> 30% of each run, Pallas kernels for 0% -> 0%
where the time goes in v1:
time: 271 us; the launch traced here: 270 us
  waiting for transfers between devices  118 us (44%)
  matrix products  71.3 us (26%)
  blocking collectives  27.1 us (10%)
  starting transfers between devices  19.5 us (7%)
  between operations  16.7 us (6%)
  local copies, waits for them, and re-layouts  9.43 us (3%)
  other arithmetic  7.85 us (3%)
    all_gather x1, waiting for transfers between devices, body(): lax.all_gather(conv_out_weight, ('fsdp', 'seq'), axis=1, tiled=True)  65.5 us
    dot_general x3, matrix products, block_product(): return jnp.dot(left_rows, right_matrix, preferred_element_type=jnp.float32)  60.5 us
    all_gather x1, waiting for transfers between devices, body(): lax.all_gather(conv_in_weight, ('fsdp', 'seq'), axis=1, tiled=True)  52 us
    psum x1, blocking collectives, body(): numerator = lax.psum(jnp.sum(frame_error), 'seq')  16.7 us
    all_to_all x1, starting transfers between devices, body(): lax.all_to_all(jnp.stack([head_weight] * lax.axis_size(('fsdp', 'seq'))),...  13.6 us
    psum x1, blocking collectives, body(): frame_error = lax.psum(frame_err, 'seed') / jnp.float32(seed_count)  10.4 us
    dot_general x1, matrix products, body(): jnp.dot(blocks, stem_matrix[:half_width], preferred_element_type=jnp.floa...  5.66 us
  transfers between devices with their start and end apart: 6, of which 2 were waited for; matrix products, arithmetic and copies ran while one was open for 30% of the time, Pallas kernels for 0%

profile of v1, /device:TPU:8, one launch (start us, length us, event | category | flops | bytes accessed | tf_op | source)
XLA Modules:
  0.0 270.3 jit_solution(12807974931611391984)
XLA Ops:
  7.2 0.0 copy-start
  7.2 0.0 all-gather.3.cloned.1.call-start
  7.2 0.7 all-gather.3.cloned.1.call-update
  7.9 0.0 all-gather.5.cloned.1.call-start
  8.0 1.5 copy.22
  9.4 0.0 all-gather.5.cloned.1.call-update
  9.5 0.7 slice.261
  10.2 0.1 copy.21
  10.3 0.1 slice.262
  10.4 1.3 collective-permute-start
  11.7 2.0 stack.2
  13.7 0.0 copy-start.3
  13.7 0.0 copy-start.2
  13.7 13.6 %all-to-all-start = ((bf16[64,1,24,512]{3,2,1,0:T(8,128)(2,1)}), bf16[64,1,24,512]{3,2,1,0:T(8,128)(2,1)}, u32[]{:S(2)}, u32[]{:S(2)}) async-start(bf16[64,1,24,512]{3,2,1,0:T(8,128)(2,1)} %stack.2), calls=%async_computation | async-start | bytes 3145728 | tf_op jit(solution)/shard_map/all_to_all | solution.py:97
  27.3 0.0 copy-done
  27.3 0.6 copy.19
  28.0 0.7 reshape_squeeze.3
  29.3 0.0 copy-done.3
  29.4 0.0 copy-done.2
  29.4 0.2 convert_reduce_fusion.31
  29.5 5.7 %fusion.53 = f32[1024,1536]{1,0:T(8,128)} fusion(bf16[1024,320]{1,0:T(8,128)(2,1)S(1)} %reshape_squeeze.3, bf16[1,640,1536]{2,1,0:T(8,128)(2,1)} %param.14), kind=kOutput, calls=%fused_computation.109 | convolution fusion | flops 1006632960 | bytes 7929856 | tf_op jit(solution)/shard_map/dot_general | solution.py:60
  35.2 0.2 slice.259
  35.4 0.6 copy.20
  36.1 1.6 slice.260
  37.7 0.0 collective-permute-done
  37.7 5.2 %convert_reduce_fusion = (f32[1024]{0:T(1024)S(1)}, bf16[1024,1536]{1,0:T(8,128)(2,1)S(1)}) fusion(f32[1024,1536]{1,0:T(8,128)} %fusion.53, bf16[1,640,1536]{2,1,0:T(8,128)(2,1)} %param.14, bf16[1,320]{1,0:T(2,128)(2,1)S(1)} %collective-permute-done, bf16[1023,320]{1,0:T(8,128)(2,1)} %slice.260), kind=kOutput, calls=%fused_computation.2 | convolution fusion | flops 1014234112 | bytes 11211392 | tf_op jit(solution)/shard_map/dot_general | solution.py:61
  42.9 1.0 fusion.2
  43.9 52.0 %all-gather.3.cloned.1.call-done = bf16[1,1536,1536]{2,1,0:T(8,128)(2,1)} async-done(((bf16[1,24,1536]{2,1,0:T(8,128)(2,1)}), bf16[1,1536,1536]{2,1,0:T(8,128)(2,1)}) %all-gather.3.cloned.1.call-update) | async-done | bytes 4718608 | tf_op jit(solution)/shard_map/all_gather | solution.py:73
  95.9 7.2 %fusion.5 = f32[1024,1536]{1,0:T(8,128)S(1)} fusion(bf16[1,1536,1536]{2,1,0:T(8,128)(2,1)} %all-gather.3.cloned.1.call-done, bf16[1024,1536]{1,0:T(8,128)(2,1)S(1)} %get-tuple-element.40, f32[1536]{0:T(1024)S(1)} %get-tuple-element.34, f32[1024]{0:T(1024)S(1)} %add_rsqrt_fusion.1, f32[1024]{0:T(1024)S(1)} %broadcast_multiply_fusion.2), kind=kOutput, calls=%fused_computation.39 | convolution fusion | flops 4839702528 | bytes 14170112 | tf_op jit(solution)/shard_map/dot_general | solution.py:34
  103.2 0.0 copy-start.5
  103.2 0.8 fusion.20
  104.1 0.0 copy-start.1
  104.1 1.1 copy-done.1
  105.2 3.1 %collective-permute-start.1 = (bf16[15,768]{1,0:T(8,128)(2,1)S(1)}, bf16[15,768]{1,0:T(8,128)(2,1)S(1)}, u32[]{:S(2)}, u32[]{:S(2)}) collective-permute-start(bf16[15,768]{1,0:T(8,128)(2,1)S(1)} %get-tuple-element.35), channel_id=1, source_target_pairs={{0,1},{1,2},{2,3},{3,4},{4,5},{5,6},{6,7},{8,9},{9,10},{10,11},{11... | collective-permute-start | bytes 69128 | tf_op jit(solution)/shard_map/ppermute | solution.py:20
  108.3 1.5 collective-permute-start.2
  109.8 0.1 convert_reduce_fusion.30
  109.9 0.0 copy-done.5
  109.9 65.5 %all-gather.5.cloned.1.call-done = bf16[1,768,1536]{2,0,1:T(2,128)(2,1)} async-done(((bf16[1,12,1536]{2,0,1:T(2,128)(2,1)}), bf16[1,768,1536]{2,0,1:T(2,128)(2,1)}) %all-gather.5.cloned.1.call-update) | async-done | bytes 2359312 | tf_op jit(solution)/shard_map/all_gather | solution.py:90
  175.5 0.0 collective-permute-done.1
  175.5 0.0 collective-permute-done.2
  175.5 48.2 %fusion.69 = (f32[1024]{0:T(1024)S(1)}, f32[1024,1536]{1,0:T(8,128)}) fusion(bf16[1,768,1536]{2,0,1:T(2,128)(2,1)} %all-gather.5.cloned.1.call-done, bf16[1024,768]{1,0:T(8,128)(2,1)} %copy-done.1, bf16[15,768]{1,0:T(8,128)(2,1)S(1)} %collective-permute-done.2, bf16[15,768]{1,0:T(8,128)(2,1)S(1)} %collective-permute-done.1, ...), kind=kOutput, calls=%fused_computation.165 | convolution fusion | flops 2567699456 | bytes 13514752 | tf_op jit(solution)/shard_map/dot_general | solution.py:34
  223.7 3.5 %multiply_reduce_fusion = f32[1024]{0:T(1024)S(1)} fusion(f32[1024,1536]{1,0:T(8,128)} %get-tuple-element.42, f32[1024]{0:T(1024)S(1)} %broadcast_multiply_fusion.1), kind=kLoop, calls=%fused_computation.37 | loop fusion | flops 4717568 | bytes 6299648 | tf_op jit(solution)/shard_map/reduce_sum | solution.py:29
  227.2 0.0 all-to-all-done
  227.2 0.0 copy-start.4
  227.3 5.0 %fusion.70 = (f32[1024]{0:T(1024)S(1)}, f32[1024,512]{0,1:T(8,128)S(1)}) fusion(bf16[1536,512]{1,0:T(8,128)(2,1)} %bitcast.5, f32[1024,1536]{1,0:T(8,128)} %get-tuple-element.42, f32[1536]{0:T(1024)S(1)} %get-tuple-element.33, f32[1024]{0:T(1024)S(1)} %add_rsqrt_fusion, f32[1024]{0:T(1024)S(1)} %broadcast_multiply_fusion.1), kind=kOutput, calls=%fused_computation.166 | convolution fusion | flops 1617427456 | bytes 9979904 | tf_op jit(solution)/shard_map/dot_general | solution.py:34
  232.3 0.3 fusion.23
  232.6 0.0 copy-done.4
  232.6 0.7 multiply_reduce_fusion.1
  233.3 10.4 %psum.14 = f32[1024]{0:T(1024)S(1)} all-reduce(f32[1024]{0:T(1024)S(1)} %select_multiply_fusion), channel_id=1, replica_groups=mesh['seed'=4,'fsdp'=8,'seq'=8] {'seed'}, use_global_device_ids=true, to_apply=%region_7.8 | all-reduce | flops 1024 | bytes 8192 | tf_op jit(solution)/shard_map/psum | solution.py:115
  243.7 1.2 fusion.67
  244.9 16.7 %psum.15 = f32[]{:T(128)} all-reduce(f32[]{:T(128)} %get-tuple-element.37), channel_id=1, replica_groups=mesh['seed'=4,'fsdp'=8,'seq'=8] {'seq'}, use_global_device_ids=true, to_apply=%region_9.10 | all-reduce | flops 1 | bytes 8 | tf_op jit(solution)/shard_map/psum | solution.py:116
  (9 shorter events, 0.1 us)
Async XLA Ops:
  7.2 20.1 %copy-start = (bf16[1,4096,80]{1,2,0:T(8,128)(2,1)S(1)}, bf16[1,4096,80]{1,2,0:T(8,128)(2,1)}, u32[]{:S(2)}) copy-start(bf16[1,4096,80]{1,2,0:T(8,128)(2,1)} %param.10) | copy-start | bytes 1966084
  7.2 88.8 %all-gather.3.cloned.1.call-start = ((), (), s32[]{:S(2)}) async-start(), calls=%async_computation.1 | async-start | bytes 4792320 | tf_op jit(solution)/shard_map/all_gather | solution.py:73
  7.9 167.6 %all-gather.5.cloned.1.call-start = ((), (), s32[]{:S(2)}) async-start(), calls=%async_computation.2 | async-start | bytes 4792320 | tf_op jit(solution)/shard_map/all_gather | solution.py:90
  10.4 27.3 %collective-permute-start = (bf16[1,320]{1,0:T(2,128)(2,1)S(1)}, bf16[1,320]{1,0:T(2,128)(2,1)S(1)}, u32[]{:S(2)}, u32[]{:S(2)}) collective-permute-start(bf16[1,320]{1,0:T(2,128)(2,1)S(1)} %slice.262), channel_id=1, source_target_pairs={{1,0},{2,1},{3,2},{4,3},{5,4},{6,5},{7,6},{9,8},{10,9},{11,10},{12... | collective-permute-start | bytes 1928 | tf_op jit(solution)/shard_map/ppermute | solution.py:10
  13.7 15.6 %copy-start.3 = (f32[1,2,1536]{2,1,0:T(2,128)S(1)}, f32[1,2,1536]{2,1,0:T(2,128)}, u32[]{:S(2)}) copy-start(f32[1,2,1536]{2,1,0:T(2,128)} %param.19) | copy-start | bytes 36868
  13.7 15.7 %copy-start.2 = (bf16[1,31,768]{2,1,0:T(8,128)(2,1)S(1)}, bf16[1,31,768]{2,1,0:T(8,128)(2,1)}, u32[]{:S(2)}) copy-start(bf16[1,31,768]{2,1,0:T(8,128)(2,1)} %param.17) | copy-start | bytes 142852
  13.7 213.5 %all-to-all-start = ((bf16[64,1,24,512]{3,2,1,0:T(8,128)(2,1)}), bf16[64,1,24,512]{3,2,1,0:T(8,128)(2,1)}, u32[]{:S(2)}, u32[]{:S(2)}) async-start(bf16[64,1,24,512]{3,2,1,0:T(8,128)(2,1)} %stack.2), calls=%async_computation | async-start | bytes 3145728 | tf_op jit(solution)/shard_map/all_to_all | solution.py:97
  103.2 6.7 %copy-start.5 = (s32[1,1024]{1,0:T(1,128)S(1)}, s32[1,1024]{1,0:T(1,128)}, u32[]{:S(2)}) copy-start(s32[1,1024]{1,0:T(1,128)} %param.13) | copy-start | bytes 12292
  104.1 1.1 copy-start.1
  105.2 70.3 %collective-permute-start.1 = (bf16[15,768]{1,0:T(8,128)(2,1)S(1)}, bf16[15,768]{1,0:T(8,128)(2,1)S(1)}, u32[]{:S(2)}, u32[]{:S(2)}) collective-permute-start(bf16[15,768]{1,0:T(8,128)(2,1)S(1)} %get-tuple-element.35), channel_id=1, source_target_pairs={{0,1},{1,2},{2,3},{3,4},{4,5},{5,6},{6,7},{8,9},{9,10},{10,11},{11... | collective-permute-start | bytes 69128 | tf_op jit(solution)/shard_map/ppermute | solution.py:20
  108.3 67.2 %collective-permute-start.2 = (bf16[15,768]{1,0:T(8,128)(2,1)S(1)}, bf16[15,768]{1,0:T(8,128)(2,1)S(1)}, u32[]{:S(2)}, u32[]{:S(2)}) collective-permute-start(bf16[15,768]{1,0:T(8,128)(2,1)S(1)} %get-tuple-element.36), channel_id=1, source_target_pairs={{1,0},{2,1},{3,2},{4,3},{5,4},{6,5},{7,6},{9,8},{10,9},{11,10},{12... | collective-permute-start | bytes 69128 | tf_op jit(solution)/shard_map/ppermute | solution.py:21
  227.2 5.4 %copy-start.4 = (s32[1,1024]{1,0:T(1,128)S(1)}, s32[1,1024]{1,0:T(1,128)}, u32[]{:S(2)}) copy-start(s32[1,1024]{1,0:T(1,128)} %param.12) | copy-start | bytes 12292
Sparse Core Ops, SparseCore 0:
  10.8 85.1 all-gather.2
  98.7 76.7 all-gather.4
